TPU v7x, 512 devices: a whole 4x8x8 slice. The times are simulated.
512 devices in a mesh: bias: 8 (over z_lo, x), gx: 8 (over z_hi, core), gy: 8 (over y).
Axes of the slice: x: 4, y: 8, z: 8 (z_hi: 4, z_lo: 2; z = z_hi * 2 + z_lo), core: 2. Of those that a mesh axis runs over, the one named last changes fastest.
Arguments:
- source: bfloat16 [8, 16, 24, 32, 256], P('bias', 'gx', 'gy'), may hold values from -6 to 6
- inverse: bfloat16 [8, 16, 24, 256, 256], P('bias', 'gx', 'gy'), may hold values from -0.375 to 0.375
- coupling: bfloat16 [8, 16, 24, 4, 256, 256], P('bias', 'gx', 'gy'), may hold values from -0.1875 to 0.1875
- sensitivity: float32 [8, 16, 24, 256], P('bias', 'gx', 'gy'), may hold values from -6 to 6
Outputs:
- adjoint_out: bfloat16 [8, 16, 24, 32, 256], P('bias', 'gx', 'gy')
- doping_grad: float32 [16, 24, 2048], P('gx', 'gy', 'bias')
All inputs are finite; a program needn't handle non-finite values.
Results may differ from a plain program's by a relative error of at most 0.02.
Values may be sent and summed in bfloat16 or wider, within the bound.
A program may use at most 64 MiB of HBM per device.

v0:
```python
import jax
import jax.numpy as jnp
from jax import lax
from jax.sharding import PartitionSpec as P

VARS = 4
ITERS = 3


def shifted(block, axis, distance):
    devices = range(lax.axis_size(axis))
    route = [(i - distance, i) for i in devices if i - distance in devices]
    return lax.ppermute(block, axis, route)


def shards(source, inverse, coupling, sensitivity):
    source_b = source[0]
    inverse_b = inverse[0]
    coupling_b = coupling[0]
    source_f = source_b.astype(jnp.float32)
    adjoint = jnp.einsum(
        "xyru,xyuv->xyrv", source_b, inverse_b, preferred_element_type=jnp.float32
    ).astype(jnp.bfloat16)
    for step in range(ITERS):
        products = jnp.einsum(
            "xyru,xyduv->xydrv", adjoint, coupling_b, preferred_element_type=jnp.float32
        ).astype(jnp.bfloat16)
        west_part = shifted(products[-1:, :, 0], "gx", 1)
        east_part = shifted(products[:1, :, 1], "gx", -1)
        south_part = shifted(products[:, -1:, 2], "gy", 1)
        north_part = shifted(products[:, :1, 3], "gy", -1)
        plus_x = jnp.concatenate([west_part, products[:-1, :, 0]], axis=0)
        minus_x = jnp.concatenate([products[1:, :, 1], east_part], axis=0)
        plus_y = jnp.concatenate([south_part, products[:, :-1, 2]], axis=1)
        minus_y = jnp.concatenate([products[:, 1:, 3], north_part], axis=1)
        incoming = (
            plus_x.astype(jnp.float32)
            + minus_x.astype(jnp.float32)
            + plus_y.astype(jnp.float32)
            + minus_y.astype(jnp.float32)
        )
        update = (source_f - incoming).astype(jnp.bfloat16)
        adjoint = jnp.einsum(
            "xyru,xyuv->xyrv", update, inverse_b, preferred_element_type=jnp.float32
        ).astype(jnp.bfloat16)
    blocks_x = adjoint.shape[0]
    blocks_y = adjoint.shape[1]
    sides = adjoint.shape[2]
    width = adjoint.shape[3] // VARS
    shaped = adjoint.astype(jnp.float32).reshape(blocks_x, blocks_y, sides, VARS, width)
    weights = sensitivity[0].reshape(blocks_x, blocks_y, 1, VARS, width)
    terms = jnp.sum(shaped * weights, axis=3).reshape(blocks_x, blocks_y, sides * width)
    summed = lax.psum(terms.astype(jnp.bfloat16), "bias").astype(jnp.float32)
    share = summed.shape[2] // lax.axis_size("bias")
    doping_grad = lax.dynamic_slice_in_dim(summed, lax.axis_index("bias") * share, share, 2)
    return (adjoint[None], doping_grad)


def solution(mesh):
    placed = (
        P("bias", "gx", "gy", None, None),
        P("bias", "gx", "gy", None, None),
        P("bias", "gx", "gy", None, None, None),
        P("bias", "gx", "gy", None),
    )
    return jax.shard_map(
        shards,
        mesh=mesh,
        in_specs=placed,
        out_specs=(P("bias", "gx", "gy", None, None), P("gx", "gy", "bias")),
        check_vma=False,
    )
```

profile of v0, /device:TPU:272, one launch (start us, length us, event | category | flops | bytes accessed | tf_op | source)
XLA Modules:
  0.0 102.6 jit_solution(6495505845985194345)
XLA Ops:
  0.6 0.0 copy-start
  0.6 1.9 %copy-done = bf16[1,2,3,4,256,256]{5,4,3,2,1,0:T(8,128)(2,1)S(1)} copy-done((bf16[1,2,3,4,256,256]{5,4,3,2,1,0:T(8,128)(2,1)S(1)}, bf16[1,2,3,4,256,256]{5,4,3,2,1,0:T(8,128)(2,1)}, u32[]{:S(2)}) %copy-start) | copy-done | bytes 3145752
  2.5 2.0 %fusion.10 = bf16[2,3,4,32,256]{4,3,2,1,0:T(8,128)(2,1)S(1)} fusion(bf16[1,2,3,256,256]{4,3,2,1,0:T(8,128)(2,1)} %param.5, bf16[1,2,3,32,256]{4,3,2,1,0:T(8,128)(2,1)} %param.4, bf16[1,2,3,4,256,256]{5,4,3,2,1,0:T(8,128)(2,1)S(1)} %copy-done), kind=kOutput, calls=%fused_computation.7 | convolution fusion | flops 126074880 | bytes 4423680 | tf_op jit(solution)/shard_map/xyru,xyduv->xydrv/dot_general | solution.py:25
  4.5 0.7 slice_bitcast_fusion.15
  5.2 1.9 %collective-permute-start = (bf16[1,3,32,256]{3,2,1,0:T(8,128)(2,1)}, bf16[1,3,32,256]{3,2,1,0:T(8,128)(2,1)}, u32[]{:S(2)}, u32[]{:S(2)}) collective-permute-start(bf16[1,3,32,256]{3,2,1,0:T(8,128)(2,1)} %get-tuple-element.24), channel_id=1, source_target_pairs={{0,8},{8,16},{16,24},{24,32},{32,40},{40,48},{48,56},{1,9},{9,17},... | collective-permute-start | bytes 147464 | tf_op jit(solution)/shard_map/ppermute | solution.py:13
  7.1 5.8 %collective-permute-start.1 = (bf16[1,3,32,256]{3,2,1,0:T(8,128)(2,1)}, bf16[1,3,32,256]{3,2,1,0:T(8,128)(2,1)}, u32[]{:S(2)}, u32[]{:S(2)}) collective-permute-start(bf16[1,3,32,256]{3,2,1,0:T(8,128)(2,1)} %get-tuple-element.25), channel_id=1, source_target_pairs={{8,0},{16,8},{24,16},{32,24},{40,32},{48,40},{56,48},{9,1},{17,9},... | collective-permute-start | bytes 147464 | tf_op jit(solution)/shard_map/ppermute | solution.py:13
  12.9 0.6 slice_bitcast_fusion.22
  13.5 2.3 %collective-permute-start.3 = (bf16[2,1,32,256]{3,2,0,1:T(8,128)(2,1)}, bf16[2,1,32,256]{3,2,0,1:T(8,128)(2,1)}, u32[]{:S(2)}, u32[]{:S(2)}) collective-permute-start(bf16[2,1,32,256]{3,2,0,1:T(8,128)(2,1)} %get-tuple-element.20), channel_id=1, source_target_pairs={{1,0},{2,1},{3,2},{4,3},{5,4},{6,5},{7,6},{9,8},{10,9},{11,10},{12... | collective-permute-start | bytes 98312 | tf_op jit(solution)/shard_map/ppermute | solution.py:13
  15.9 3.5 %collective-permute-start.2 = (bf16[2,1,32,256]{3,2,1,0:T(8,128)(2,1)}, bf16[2,1,32,256]{3,2,1,0:T(8,128)(2,1)}, u32[]{:S(2)}, u32[]{:S(2)}) collective-permute-start(bf16[2,1,32,256]{3,2,1,0:T(8,128)(2,1)} %get-tuple-element.21), channel_id=1, source_target_pairs={{0,1},{1,2},{2,3},{3,4},{4,5},{5,6},{6,7},{8,9},{9,10},{10,11},{11... | collective-permute-start | bytes 98312 | tf_op jit(solution)/shard_map/ppermute | solution.py:13
  19.4 0.7 slice_bitcast_fusion.4
  20.0 0.8 mul.13
  20.8 1.2 %collective-permute-done.2 = bf16[2,1,32,256]{3,2,1,0:T(8,128)(2,1)} collective-permute-done((bf16[2,1,32,256]{3,2,1,0:T(8,128)(2,1)}, bf16[2,1,32,256]{3,2,1,0:T(8,128)(2,1)}, u32[]{:S(2)}, u32[]{:S(2)}) %collective-permute-start.2) | collective-permute-done | bytes 32800 | tf_op jit(solution)/shard_map/ppermute | solution.py:13
  22.0 1.6 %fusion.18 = bf16[2,3,32,256,1]{3,2,1,0,4:T(8,128)(2,1)S(1)} fusion(bf16[1,2,3,256,256]{4,3,2,1,0:T(8,128)(2,1)} %param.5, bf16[1,3,32,256]{3,2,1,0:T(8,128)(2,1)} %get-tuple-element.23, bf16[1,3,32,256]{3,2,1,0:T(8,128)(2,1)} %collective-permute-done, bf16[1,3,32,256]{3,2,1,0:T(8,128)(2,1)} %collective-permute-done.1, ...), kind=kOutput, calls=%fused_computation.15 | convolution fusion | flops 25903104 | bytes 1376256 | tf_op jit(solution)/shard_map/xyru,xyuv->xyrv/dot_general | solution.py:43
  23.6 0.7 fusion.14
  24.3 2.1 %collective-permute-start.4 = (bf16[1,3,32,256]{3,2,0,1:T(8,128)(2,1)S(1)}, bf16[1,3,32,256]{3,2,0,1:T(8,128)(2,1)S(1)}, u32[]{:S(2)}, u32[]{:S(2)}) collective-permute-start(bf16[1,3,32,256]{3,2,0,1:T(8,128)(2,1)S(1)} %get-tuple-element.16), channel_id=1, source_target_pairs={{0,8},{8,16},{16,24},{24,32},{32,40},{40,48},{48,56},{1,9},{9,17},... | collective-permute-start | bytes 147464 | tf_op jit(solution)/shard_map/ppermute | solution.py:13
  26.4 5.8 %collective-permute-start.5 = (bf16[1,3,32,256]{3,2,0,1:T(8,128)(2,1)S(1)}, bf16[1,3,32,256]{3,2,0,1:T(8,128)(2,1)S(1)}, u32[]{:S(2)}, u32[]{:S(2)}) collective-permute-start(bf16[1,3,32,256]{3,2,0,1:T(8,128)(2,1)S(1)} %get-tuple-element.17), channel_id=1, source_target_pairs={{8,0},{16,8},{24,16},{32,24},{40,32},{48,40},{56,48},{9,1},{17,9},... | collective-permute-start | bytes 147464 | tf_op jit(solution)/shard_map/ppermute | solution.py:13
  32.2 4.0 %collective-permute-start.6 = (bf16[2,1,32,256]{3,2,0,1:T(8,128)(2,1)S(1)}, bf16[2,1,32,256]{3,2,0,1:T(8,128)(2,1)S(1)}, u32[]{:S(2)}, u32[]{:S(2)}) collective-permute-start(bf16[2,1,32,256]{3,2,0,1:T(8,128)(2,1)S(1)} %get-tuple-element.13), channel_id=1, source_target_pairs={{0,1},{1,2},{2,3},{3,4},{4,5},{5,6},{6,7},{8,9},{9,10},{10,11},{11... | collective-permute-start | bytes 98312 | tf_op jit(solution)/shard_map/ppermute | solution.py:13
  36.1 1.9 %collective-permute-start.7 = (bf16[2,1,32,256]{3,2,1,0:T(8,128)(2,1)S(1)}, bf16[2,1,32,256]{3,2,1,0:T(8,128)(2,1)S(1)}, u32[]{:S(2)}, u32[]{:S(2)}) collective-permute-start(bf16[2,1,32,256]{3,2,1,0:T(8,128)(2,1)S(1)} %get-tuple-element.12), channel_id=1, source_target_pairs={{1,0},{2,1},{3,2},{4,3},{5,4},{6,5},{7,6},{9,8},{10,9},{11,10},{12... | collective-permute-start | bytes 98312 | tf_op jit(solution)/shard_map/ppermute | solution.py:13
  38.1 5.4 %collective-permute-done.7 = bf16[2,1,32,256]{3,2,1,0:T(8,128)(2,1)S(1)} collective-permute-done((bf16[2,1,32,256]{3,2,1,0:T(8,128)(2,1)S(1)}, bf16[2,1,32,256]{3,2,1,0:T(8,128)(2,1)S(1)}, u32[]{:S(2)}, u32[]{:S(2)}) %collective-permute-start.7) | collective-permute-done | bytes 32800 | tf_op jit(solution)/shard_map/ppermute | solution.py:13
  43.5 1.1 %fusion.19 = bf16[2,3,32,256,1]{3,2,1,0,4:T(8,128)(2,1)S(1)} fusion(bf16[1,2,3,256,256]{4,3,2,1,0:T(8,128)(2,1)S(1)} %copy-done.1, bf16[2,1,32,256]{3,2,1,0:T(8,128)(2,1)S(1)} %collective-permute-done.7, bf16[1,2,3,32,256]{4,3,2,1,0:T(8,128)(2,1)} %param.4, bf16[1,3,32,256]{3,2,0,1:T(8,128)(2,1)S(1)} %get-tuple-element.15, ...), kind=kOutput, calls=%fused_computation.16 | convolution fusion | flops 26001408 | bytes 1376256 | tf_op jit(solution)/shard_map/xyru,xyuv->xyrv/dot_general | solution.py:43
  44.6 0.7 fusion.11
  45.3 1.9 %collective-permute-start.8 = (bf16[1,3,32,256]{3,2,0,1:T(8,128)(2,1)S(1)}, bf16[1,3,32,256]{3,2,0,1:T(8,128)(2,1)S(1)}, u32[]{:S(2)}, u32[]{:S(2)}) collective-permute-start(bf16[1,3,32,256]{3,2,0,1:T(8,128)(2,1)S(1)} %get-tuple-element.8), channel_id=1, source_target_pairs={{0,8},{8,16},{16,24},{24,32},{32,40},{40,48},{48,56},{1,9},{9,17},... | collective-permute-start | bytes 147464 | tf_op jit(solution)/shard_map/ppermute | solution.py:13
  47.2 5.8 %collective-permute-start.9 = (bf16[1,3,32,256]{3,2,0,1:T(8,128)(2,1)S(1)}, bf16[1,3,32,256]{3,2,0,1:T(8,128)(2,1)S(1)}, u32[]{:S(2)}, u32[]{:S(2)}) collective-permute-start(bf16[1,3,32,256]{3,2,0,1:T(8,128)(2,1)S(1)} %get-tuple-element.9), channel_id=1, source_target_pairs={{8,0},{16,8},{24,16},{32,24},{40,32},{48,40},{56,48},{9,1},{17,9},... | collective-permute-start | bytes 147464 | tf_op jit(solution)/shard_map/ppermute | solution.py:13
  53.0 5.1 %collective-permute-start.10 = (bf16[2,1,32,256]{3,2,0,1:T(8,128)(2,1)S(1)}, bf16[2,1,32,256]{3,2,0,1:T(8,128)(2,1)S(1)}, u32[]{:S(2)}, u32[]{:S(2)}) collective-permute-start(bf16[2,1,32,256]{3,2,0,1:T(8,128)(2,1)S(1)} %get-tuple-element.5), channel_id=1, source_target_pairs={{0,1},{1,2},{2,3},{3,4},{4,5},{5,6},{6,7},{8,9},{9,10},{10,11},{11... | collective-permute-start | bytes 98312 | tf_op jit(solution)/shard_map/ppermute | solution.py:13
  58.1 1.9 %collective-permute-start.11 = (bf16[2,1,32,256]{3,2,1,0:T(8,128)(2,1)S(1)}, bf16[2,1,32,256]{3,2,1,0:T(8,128)(2,1)S(1)}, u32[]{:S(2)}, u32[]{:S(2)}) collective-permute-start(bf16[2,1,32,256]{3,2,1,0:T(8,128)(2,1)S(1)} %get-tuple-element.4), channel_id=1, source_target_pairs={{1,0},{2,1},{3,2},{4,3},{5,4},{6,5},{7,6},{9,8},{10,9},{11,10},{12... | collective-permute-start | bytes 98312 | tf_op jit(solution)/shard_map/ppermute | solution.py:13
  60.1 3.9 %collective-permute-done.11 = bf16[2,1,32,256]{3,2,1,0:T(8,128)(2,1)S(1)} collective-permute-done((bf16[2,1,32,256]{3,2,1,0:T(8,128)(2,1)S(1)}, bf16[2,1,32,256]{3,2,1,0:T(8,128)(2,1)S(1)}, u32[]{:S(2)}, u32[]{:S(2)}) %collective-permute-start.11) | collective-permute-done | bytes 32800 | tf_op jit(solution)/shard_map/ppermute | solution.py:13
  64.0 0.9 convolution_convert_fusion.1
  64.9 1.1 %reshape.16 = f32[2,3,32,4,64]{4,3,2,1,0:T(4,128)S(1)} reshape(bf16[2,3,32,256]{3,2,1,0:T(8,128)(2,1)} %convolution_convert_fusion.1) | data formatting | bytes 294912 | tf_op jit(solution)/shard_map/reshape | solution.py:50
  66.0 0.9 multiply_reduce_fusion
  66.9 0.9 reshape.20
  67.8 34.2 %psum.7 = bf16[2,3,2048]{2,0,1:T(2,128)(2,1)S(1)} all-reduce(bf16[2,3,2048]{2,0,1:T(2,128)(2,1)S(1)} %copy.80), channel_id=1, replica_groups=mesh['bias'=8,'gx'=8,'gy'=8] {'bias'}, use_global_device_ids=true, to_apply=%region_1.0 | all-reduce | flops 12288 | bytes 49152 | tf_op jit(solution)/shard_map/psum | solution.py:53
  102.0 0.6 dynamic-slice_convert_fusion
  (20 shorter events, 0.1 us)
Async XLA Ops:
  0.6 1.9 %copy-start = (bf16[1,2,3,4,256,256]{5,4,3,2,1,0:T(8,128)(2,1)S(1)}, bf16[1,2,3,4,256,256]{5,4,3,2,1,0:T(8,128)(2,1)}, u32[]{:S(2)}) copy-start(bf16[1,2,3,4,256,256]{5,4,3,2,1,0:T(8,128)(2,1)} %param.6) | copy-start | bytes 9437188
  5.2 16.8 %collective-permute-start = (bf16[1,3,32,256]{3,2,1,0:T(8,128)(2,1)}, bf16[1,3,32,256]{3,2,1,0:T(8,128)(2,1)}, u32[]{:S(2)}, u32[]{:S(2)}) collective-permute-start(bf16[1,3,32,256]{3,2,1,0:T(8,128)(2,1)} %get-tuple-element.24), channel_id=1, source_target_pairs={{0,8},{8,16},{16,24},{24,32},{32,40},{40,48},{48,56},{1,9},{9,17},... | collective-permute-start | bytes 147464 | tf_op jit(solution)/shard_map/ppermute | solution.py:13
  7.1 14.9 %collective-permute-start.1 = (bf16[1,3,32,256]{3,2,1,0:T(8,128)(2,1)}, bf16[1,3,32,256]{3,2,1,0:T(8,128)(2,1)}, u32[]{:S(2)}, u32[]{:S(2)}) collective-permute-start(bf16[1,3,32,256]{3,2,1,0:T(8,128)(2,1)} %get-tuple-element.25), channel_id=1, source_target_pairs={{8,0},{16,8},{24,16},{32,24},{40,32},{48,40},{56,48},{9,1},{17,9},... | collective-permute-start | bytes 147464 | tf_op jit(solution)/shard_map/ppermute | solution.py:13
  13.5 7.3 %collective-permute-start.3 = (bf16[2,1,32,256]{3,2,0,1:T(8,128)(2,1)}, bf16[2,1,32,256]{3,2,0,1:T(8,128)(2,1)}, u32[]{:S(2)}, u32[]{:S(2)}) collective-permute-start(bf16[2,1,32,256]{3,2,0,1:T(8,128)(2,1)} %get-tuple-element.20), channel_id=1, source_target_pairs={{1,0},{2,1},{3,2},{4,3},{5,4},{6,5},{7,6},{9,8},{10,9},{11,10},{12... | collective-permute-start | bytes 98312 | tf_op jit(solution)/shard_map/ppermute | solution.py:13
  15.9 6.1 %collective-permute-start.2 = (bf16[2,1,32,256]{3,2,1,0:T(8,128)(2,1)}, bf16[2,1,32,256]{3,2,1,0:T(8,128)(2,1)}, u32[]{:S(2)}, u32[]{:S(2)}) collective-permute-start(bf16[2,1,32,256]{3,2,1,0:T(8,128)(2,1)} %get-tuple-element.21), channel_id=1, source_target_pairs={{0,1},{1,2},{2,3},{3,4},{4,5},{5,6},{6,7},{8,9},{9,10},{10,11},{11... | collective-permute-start | bytes 98312 | tf_op jit(solution)/shard_map/ppermute | solution.py:13
  20.8 22.7 %copy-start.1 = (bf16[1,2,3,256,256]{4,3,2,1,0:T(8,128)(2,1)S(1)}, bf16[1,2,3,256,256]{4,3,2,1,0:T(8,128)(2,1)}, u32[]{:S(2)}) copy-start(bf16[1,2,3,256,256]{4,3,2,1,0:T(8,128)(2,1)} %param.5) | copy-start | bytes 2359300
  24.3 39.6 %copy-start.2 = (bf16[1,2,3,32,256]{4,3,2,1,0:T(8,128)(2,1)S(1)}, bf16[1,2,3,32,256]{4,3,2,1,0:T(8,128)(2,1)}, u32[]{:S(2)}) copy-start(bf16[1,2,3,32,256]{4,3,2,1,0:T(8,128)(2,1)} %param.4) | copy-start | bytes 294916
  24.3 19.1 %collective-permute-start.4 = (bf16[1,3,32,256]{3,2,0,1:T(8,128)(2,1)S(1)}, bf16[1,3,32,256]{3,2,0,1:T(8,128)(2,1)S(1)}, u32[]{:S(2)}, u32[]{:S(2)}) collective-permute-start(bf16[1,3,32,256]{3,2,0,1:T(8,128)(2,1)S(1)} %get-tuple-element.16), channel_id=1, source_target_pairs={{0,8},{8,16},{16,24},{24,32},{32,40},{40,48},{48,56},{1,9},{9,17},... | collective-permute-start | bytes 147464 | tf_op jit(solution)/shard_map/ppermute | solution.py:13
  26.4 17.0 %collective-permute-start.5 = (bf16[1,3,32,256]{3,2,0,1:T(8,128)(2,1)S(1)}, bf16[1,3,32,256]{3,2,0,1:T(8,128)(2,1)S(1)}, u32[]{:S(2)}, u32[]{:S(2)}) collective-permute-start(bf16[1,3,32,256]{3,2,0,1:T(8,128)(2,1)S(1)} %get-tuple-element.17), channel_id=1, source_target_pairs={{8,0},{16,8},{24,16},{32,24},{40,32},{48,40},{56,48},{9,1},{17,9},... | collective-permute-start | bytes 147464 | tf_op jit(solution)/shard_map/ppermute | solution.py:13
  32.2 5.9 %collective-permute-start.6 = (bf16[2,1,32,256]{3,2,0,1:T(8,128)(2,1)S(1)}, bf16[2,1,32,256]{3,2,0,1:T(8,128)(2,1)S(1)}, u32[]{:S(2)}, u32[]{:S(2)}) collective-permute-start(bf16[2,1,32,256]{3,2,0,1:T(8,128)(2,1)S(1)} %get-tuple-element.13), channel_id=1, source_target_pairs={{0,1},{1,2},{2,3},{3,4},{4,5},{5,6},{6,7},{8,9},{9,10},{10,11},{11... | collective-permute-start | bytes 98312 | tf_op jit(solution)/shard_map/ppermute | solution.py:13
  36.1 7.3 %collective-permute-start.7 = (bf16[2,1,32,256]{3,2,1,0:T(8,128)(2,1)S(1)}, bf16[2,1,32,256]{3,2,1,0:T(8,128)(2,1)S(1)}, u32[]{:S(2)}, u32[]{:S(2)}) collective-permute-start(bf16[2,1,32,256]{3,2,1,0:T(8,128)(2,1)S(1)} %get-tuple-element.12), channel_id=1, source_target_pairs={{1,0},{2,1},{3,2},{4,3},{5,4},{6,5},{7,6},{9,8},{10,9},{11,10},{12... | collective-permute-start | bytes 98312 | tf_op jit(solution)/shard_map/ppermute | solution.py:13
  45.3 18.6 %collective-permute-start.8 = (bf16[1,3,32,256]{3,2,0,1:T(8,128)(2,1)S(1)}, bf16[1,3,32,256]{3,2,0,1:T(8,128)(2,1)S(1)}, u32[]{:S(2)}, u32[]{:S(2)}) collective-permute-start(bf16[1,3,32,256]{3,2,0,1:T(8,128)(2,1)S(1)} %get-tuple-element.8), channel_id=1, source_target_pairs={{0,8},{8,16},{16,24},{24,32},{32,40},{40,48},{48,56},{1,9},{9,17},... | collective-permute-start | bytes 147464 | tf_op jit(solution)/shard_map/ppermute | solution.py:13
  47.2 16.7 %collective-permute-start.9 = (bf16[1,3,32,256]{3,2,0,1:T(8,128)(2,1)S(1)}, bf16[1,3,32,256]{3,2,0,1:T(8,128)(2,1)S(1)}, u32[]{:S(2)}, u32[]{:S(2)}) collective-permute-start(bf16[1,3,32,256]{3,2,0,1:T(8,128)(2,1)S(1)} %get-tuple-element.9), channel_id=1, source_target_pairs={{8,0},{16,8},{24,16},{32,24},{40,32},{48,40},{56,48},{9,1},{17,9},... | collective-permute-start | bytes 147464 | tf_op jit(solution)/shard_map/ppermute | solution.py:13
  53.0 7.1 %collective-permute-start.10 = (bf16[2,1,32,256]{3,2,0,1:T(8,128)(2,1)S(1)}, bf16[2,1,32,256]{3,2,0,1:T(8,128)(2,1)S(1)}, u32[]{:S(2)}, u32[]{:S(2)}) collective-permute-start(bf16[2,1,32,256]{3,2,0,1:T(8,128)(2,1)S(1)} %get-tuple-element.5), channel_id=1, source_target_pairs={{0,1},{1,2},{2,3},{3,4},{4,5},{5,6},{6,7},{8,9},{9,10},{10,11},{11... | collective-permute-start | bytes 98312 | tf_op jit(solution)/shard_map/ppermute | solution.py:13
  58.1 5.8 %collective-permute-start.11 = (bf16[2,1,32,256]{3,2,1,0:T(8,128)(2,1)S(1)}, bf16[2,1,32,256]{3,2,1,0:T(8,128)(2,1)S(1)}, u32[]{:S(2)}, u32[]{:S(2)}) collective-permute-start(bf16[2,1,32,256]{3,2,1,0:T(8,128)(2,1)S(1)} %get-tuple-element.4), channel_id=1, source_target_pairs={{1,0},{2,1},{3,2},{4,3},{5,4},{6,5},{7,6},{9,8},{10,9},{11,10},{12... | collective-permute-start | bytes 98312 | tf_op jit(solution)/shard_map/ppermute | solution.py:13
where the time goes:
time: 103 us
  starting transfers between devices  41.9 us (41%)
  blocking collectives  34.2 us (33%)
  waiting for transfers between devices  10.4 us (10%)
  matrix products  6.95 us (7%)
  local copies, waits for them, and re-layouts  6.77 us (7%)
  other arithmetic  1.53 us (1%)
    ppermute x12, starting transfers between devices, shifted(): return lax.ppermute(block, axis, route)  41.9 us
    psum x1, blocking collectives, shards(): summed = lax.psum(terms.astype(jnp.bfloat16), 'bias').astype(jnp.float32)  34.2 us
    ppermute x12, waiting for transfers between devices, shifted(): return lax.ppermute(block, axis, route)  10.4 us
    dot_general x3, matrix products, shards(): jnp.einsum('xyru,xyuv->xyrv', update, inverse_b, preferred_element_type=j...  3.69 us
    dot_general x3, matrix products, shards(): jnp.einsum('xyru,xyduv->xydrv', adjoint, coupling_b, preferred_element_ty...  3.26 us
  transfers between devices with their start and end apart: 12, of which 3 were waited for; matrix products, arithmetic and copies ran while one was open for 2% of the time, Pallas kernels for 0%

commit v1 on v0

--- a/solution.py
+++ b/solution.py
@@ -50,7 +50,9 @@
     shaped = adjoint.astype(jnp.float32).reshape(blocks_x, blocks_y, sides, VARS, width)
     weights = sensitivity[0].reshape(blocks_x, blocks_y, 1, VARS, width)
     terms = jnp.sum(shaped * weights, axis=3).reshape(blocks_x, blocks_y, sides * width)
-    summed = lax.psum(terms.astype(jnp.bfloat16), "bias").astype(jnp.float32)
+    summed = jnp.sum(lax.all_gather(terms.astype(jnp.bfloat16), axis_name="bias"), axis=0).astype(
+        jnp.float32
+    )
     share = summed.shape[2] // lax.axis_size("bias")
     doping_grad = lax.dynamic_slice_in_dim(summed, lax.axis_index("bias") * share, share, 2)
     return (adjoint[None], doping_grad)

time: 103 us -> 97.9 us (0.950)
  blocking collectives: 34.2 us -> 28.6 us
    psum x1 -> x0, blocking collectives: 34.2 us -> none  [shards(): summed = lax.psum(terms.astype(jnp.bfloat16), 'bias').astype(jnp.float32)]
    all_gather x0 -> x1, blocking collectives: none -> 28.6 us  [shards(): lax.all_gather(terms.astype(jnp.bfloat16), axis_name='bias')]
where the time goes in v1:
time: 97.9 us; the launch traced here: 97.3 us
  starting transfers between devices  41.9 us (43%)
  blocking collectives  28.6 us (29%)
  waiting for transfers between devices  10.4 us (11%)
  matrix products  6.95 us (7%)
  local copies, waits for them, and re-layouts  6.77 us (7%)
  other arithmetic  1.72 us (2%)
    ppermute x12, starting transfers between devices, shifted(): return lax.ppermute(block, axis, route)  41.9 us
    all_gather x1, blocking collectives, shards(): lax.all_gather(terms.astype(jnp.bfloat16), axis_name='bias')  28.6 us
    ppermute x12, waiting for transfers between devices, shifted(): return lax.ppermute(block, axis, route)  10.4 us
    dot_general x3, matrix products, shards(): jnp.einsum('xyru,xyuv->xyrv', update, inverse_b, preferred_element_type=j...  3.69 us
    dot_general x3, matrix products, shards(): jnp.einsum('xyru,xyduv->xydrv', adjoint, coupling_b, preferred_element_ty...  3.26 us
  transfers between devices with their start and end apart: 12, of which 3 were waited for; matrix products, arithmetic and copies ran while one was open for 2% of the time, Pallas kernels for 0%

profile of v1, /device:TPU:272, one launch (start us, length us, event | category | flops | bytes accessed | tf_op | source)
XLA Modules:
  0.0 97.3 jit_solution(7004550485119155490)
XLA Ops:
  0.6 1.9 %copy-done = bf16[1,2,3,4,256,256]{5,4,3,2,1,0:T(8,128)(2,1)S(1)} copy-done((bf16[1,2,3,4,256,256]{5,4,3,2,1,0:T(8,128)(2,1)S(1)}, bf16[1,2,3,4,256,256]{5,4,3,2,1,0:T(8,128)(2,1)}, u32[]{:S(2)}) %copy-start) | copy-done | bytes 3145752
  2.5 2.0 %fusion.10 = bf16[2,3,4,32,256]{4,3,2,1,0:T(8,128)(2,1)S(1)} fusion(bf16[1,2,3,256,256]{4,3,2,1,0:T(8,128)(2,1)} %param.5, bf16[1,2,3,32,256]{4,3,2,1,0:T(8,128)(2,1)} %param.4, bf16[1,2,3,4,256,256]{5,4,3,2,1,0:T(8,128)(2,1)S(1)} %copy-done), kind=kOutput, calls=%fused_computation.7 | convolution fusion | flops 126074880 | bytes 4423680 | tf_op jit(solution)/shard_map/xyru,xyduv->xydrv/dot_general | solution.py:25
  4.5 0.7 slice_bitcast_fusion.15
  5.2 1.9 %collective-permute-start = (bf16[1,3,32,256]{3,2,1,0:T(8,128)(2,1)}, bf16[1,3,32,256]{3,2,1,0:T(8,128)(2,1)}, u32[]{:S(2)}, u32[]{:S(2)}) collective-permute-start(bf16[1,3,32,256]{3,2,1,0:T(8,128)(2,1)} %get-tuple-element.24), channel_id=1, source_target_pairs={{0,8},{8,16},{16,24},{24,32},{32,40},{40,48},{48,56},{1,9},{9,17},... | collective-permute-start | bytes 147464 | tf_op jit(solution)/shard_map/ppermute | solution.py:13
  7.1 5.8 %collective-permute-start.1 = (bf16[1,3,32,256]{3,2,1,0:T(8,128)(2,1)}, bf16[1,3,32,256]{3,2,1,0:T(8,128)(2,1)}, u32[]{:S(2)}, u32[]{:S(2)}) collective-permute-start(bf16[1,3,32,256]{3,2,1,0:T(8,128)(2,1)} %get-tuple-element.25), channel_id=1, source_target_pairs={{8,0},{16,8},{24,16},{32,24},{40,32},{48,40},{56,48},{9,1},{17,9},... | collective-permute-start | bytes 147464 | tf_op jit(solution)/shard_map/ppermute | solution.py:13
  12.9 0.6 slice_bitcast_fusion.22
  13.5 2.3 %collective-permute-start.3 = (bf16[2,1,32,256]{3,2,0,1:T(8,128)(2,1)}, bf16[2,1,32,256]{3,2,0,1:T(8,128)(2,1)}, u32[]{:S(2)}, u32[]{:S(2)}) collective-permute-start(bf16[2,1,32,256]{3,2,0,1:T(8,128)(2,1)} %get-tuple-element.20), channel_id=1, source_target_pairs={{1,0},{2,1},{3,2},{4,3},{5,4},{6,5},{7,6},{9,8},{10,9},{11,10},{12... | collective-permute-start | bytes 98312 | tf_op jit(solution)/shard_map/ppermute | solution.py:13
  15.9 3.5 %collective-permute-start.2 = (bf16[2,1,32,256]{3,2,1,0:T(8,128)(2,1)}, bf16[2,1,32,256]{3,2,1,0:T(8,128)(2,1)}, u32[]{:S(2)}, u32[]{:S(2)}) collective-permute-start(bf16[2,1,32,256]{3,2,1,0:T(8,128)(2,1)} %get-tuple-element.21), channel_id=1, source_target_pairs={{0,1},{1,2},{2,3},{3,4},{4,5},{5,6},{6,7},{8,9},{9,10},{10,11},{11... | collective-permute-start | bytes 98312 | tf_op jit(solution)/shard_map/ppermute | solution.py:13
  19.4 0.7 slice_bitcast_fusion.4
  20.0 0.8 mul.13
  20.8 1.2 %collective-permute-done.2 = bf16[2,1,32,256]{3,2,1,0:T(8,128)(2,1)} collective-permute-done((bf16[2,1,32,256]{3,2,1,0:T(8,128)(2,1)}, bf16[2,1,32,256]{3,2,1,0:T(8,128)(2,1)}, u32[]{:S(2)}, u32[]{:S(2)}) %collective-permute-start.2) | collective-permute-done | bytes 32800 | tf_op jit(solution)/shard_map/ppermute | solution.py:13
  22.0 1.6 %fusion.18 = bf16[2,3,32,256,1]{3,2,1,0,4:T(8,128)(2,1)S(1)} fusion(bf16[1,2,3,256,256]{4,3,2,1,0:T(8,128)(2,1)} %param.5, bf16[1,3,32,256]{3,2,1,0:T(8,128)(2,1)} %get-tuple-element.23, bf16[1,3,32,256]{3,2,1,0:T(8,128)(2,1)} %collective-permute-done, bf16[1,3,32,256]{3,2,1,0:T(8,128)(2,1)} %collective-permute-done.1, ...), kind=kOutput, calls=%fused_computation.15 | convolution fusion | flops 25903104 | bytes 1376256 | tf_op jit(solution)/shard_map/xyru,xyuv->xyrv/dot_general | solution.py:43
  23.6 0.7 fusion.14
  24.3 2.1 %collective-permute-start.4 = (bf16[1,3,32,256]{3,2,0,1:T(8,128)(2,1)S(1)}, bf16[1,3,32,256]{3,2,0,1:T(8,128)(2,1)S(1)}, u32[]{:S(2)}, u32[]{:S(2)}) collective-permute-start(bf16[1,3,32,256]{3,2,0,1:T(8,128)(2,1)S(1)} %get-tuple-element.16), channel_id=1, source_target_pairs={{0,8},{8,16},{16,24},{24,32},{32,40},{40,48},{48,56},{1,9},{9,17},... | collective-permute-start | bytes 147464 | tf_op jit(solution)/shard_map/ppermute | solution.py:13
  26.4 5.8 %collective-permute-start.5 = (bf16[1,3,32,256]{3,2,0,1:T(8,128)(2,1)S(1)}, bf16[1,3,32,256]{3,2,0,1:T(8,128)(2,1)S(1)}, u32[]{:S(2)}, u32[]{:S(2)}) collective-permute-start(bf16[1,3,32,256]{3,2,0,1:T(8,128)(2,1)S(1)} %get-tuple-element.17), channel_id=1, source_target_pairs={{8,0},{16,8},{24,16},{32,24},{40,32},{48,40},{56,48},{9,1},{17,9},... | collective-permute-start | bytes 147464 | tf_op jit(solution)/shard_map/ppermute | solution.py:13
  32.2 4.0 %collective-permute-start.6 = (bf16[2,1,32,256]{3,2,0,1:T(8,128)(2,1)S(1)}, bf16[2,1,32,256]{3,2,0,1:T(8,128)(2,1)S(1)}, u32[]{:S(2)}, u32[]{:S(2)}) collective-permute-start(bf16[2,1,32,256]{3,2,0,1:T(8,128)(2,1)S(1)} %get-tuple-element.13), channel_id=1, source_target_pairs={{0,1},{1,2},{2,3},{3,4},{4,5},{5,6},{6,7},{8,9},{9,10},{10,11},{11... | collective-permute-start | bytes 98312 | tf_op jit(solution)/shard_map/ppermute | solution.py:13
  36.1 1.9 %collective-permute-start.7 = (bf16[2,1,32,256]{3,2,1,0:T(8,128)(2,1)S(1)}, bf16[2,1,32,256]{3,2,1,0:T(8,128)(2,1)S(1)}, u32[]{:S(2)}, u32[]{:S(2)}) collective-permute-start(bf16[2,1,32,256]{3,2,1,0:T(8,128)(2,1)S(1)} %get-tuple-element.12), channel_id=1, source_target_pairs={{1,0},{2,1},{3,2},{4,3},{5,4},{6,5},{7,6},{9,8},{10,9},{11,10},{12... | collective-permute-start | bytes 98312 | tf_op jit(solution)/shard_map/ppermute | solution.py:13
  38.1 5.4 %collective-permute-done.7 = bf16[2,1,32,256]{3,2,1,0:T(8,128)(2,1)S(1)} collective-permute-done((bf16[2,1,32,256]{3,2,1,0:T(8,128)(2,1)S(1)}, bf16[2,1,32,256]{3,2,1,0:T(8,128)(2,1)S(1)}, u32[]{:S(2)}, u32[]{:S(2)}) %collective-permute-start.7) | collective-permute-done | bytes 32800 | tf_op jit(solution)/shard_map/ppermute | solution.py:13
  43.5 1.1 %fusion.19 = bf16[2,3,32,256,1]{3,2,1,0,4:T(8,128)(2,1)S(1)} fusion(bf16[1,2,3,256,256]{4,3,2,1,0:T(8,128)(2,1)S(1)} %copy-done.1, bf16[2,1,32,256]{3,2,1,0:T(8,128)(2,1)S(1)} %collective-permute-done.7, bf16[1,2,3,32,256]{4,3,2,1,0:T(8,128)(2,1)} %param.4, bf16[1,3,32,256]{3,2,0,1:T(8,128)(2,1)S(1)} %get-tuple-element.15, ...), kind=kOutput, calls=%fused_computation.16 | convolution fusion | flops 26001408 | bytes 1376256 | tf_op jit(solution)/shard_map/xyru,xyuv->xyrv/dot_general | solution.py:43
  44.6 0.7 fusion.11
  45.3 1.9 %collective-permute-start.8 = (bf16[1,3,32,256]{3,2,0,1:T(8,128)(2,1)S(1)}, bf16[1,3,32,256]{3,2,0,1:T(8,128)(2,1)S(1)}, u32[]{:S(2)}, u32[]{:S(2)}) collective-permute-start(bf16[1,3,32,256]{3,2,0,1:T(8,128)(2,1)S(1)} %get-tuple-element.8), channel_id=1, source_target_pairs={{0,8},{8,16},{16,24},{24,32},{32,40},{40,48},{48,56},{1,9},{9,17},... | collective-permute-start | bytes 147464 | tf_op jit(solution)/shard_map/ppermute | solution.py:13
  47.2 5.8 %collective-permute-start.9 = (bf16[1,3,32,256]{3,2,0,1:T(8,128)(2,1)S(1)}, bf16[1,3,32,256]{3,2,0,1:T(8,128)(2,1)S(1)}, u32[]{:S(2)}, u32[]{:S(2)}) collective-permute-start(bf16[1,3,32,256]{3,2,0,1:T(8,128)(2,1)S(1)} %get-tuple-element.9), channel_id=1, source_target_pairs={{8,0},{16,8},{24,16},{32,24},{40,32},{48,40},{56,48},{9,1},{17,9},... | collective-permute-start | bytes 147464 | tf_op jit(solution)/shard_map/ppermute | solution.py:13
  53.0 5.1 %collective-permute-start.10 = (bf16[2,1,32,256]{3,2,0,1:T(8,128)(2,1)S(1)}, bf16[2,1,32,256]{3,2,0,1:T(8,128)(2,1)S(1)}, u32[]{:S(2)}, u32[]{:S(2)}) collective-permute-start(bf16[2,1,32,256]{3,2,0,1:T(8,128)(2,1)S(1)} %get-tuple-element.5), channel_id=1, source_target_pairs={{0,1},{1,2},{2,3},{3,4},{4,5},{5,6},{6,7},{8,9},{9,10},{10,11},{11... | collective-permute-start | bytes 98312 | tf_op jit(solution)/shard_map/ppermute | solution.py:13
  58.1 1.9 %collective-permute-start.11 = (bf16[2,1,32,256]{3,2,1,0:T(8,128)(2,1)S(1)}, bf16[2,1,32,256]{3,2,1,0:T(8,128)(2,1)S(1)}, u32[]{:S(2)}, u32[]{:S(2)}) collective-permute-start(bf16[2,1,32,256]{3,2,1,0:T(8,128)(2,1)S(1)} %get-tuple-element.4), channel_id=1, source_target_pairs={{1,0},{2,1},{3,2},{4,3},{5,4},{6,5},{7,6},{9,8},{10,9},{11,10},{12... | collective-permute-start | bytes 98312 | tf_op jit(solution)/shard_map/ppermute | solution.py:13
  60.1 3.9 %collective-permute-done.11 = bf16[2,1,32,256]{3,2,1,0:T(8,128)(2,1)S(1)} collective-permute-done((bf16[2,1,32,256]{3,2,1,0:T(8,128)(2,1)S(1)}, bf16[2,1,32,256]{3,2,1,0:T(8,128)(2,1)S(1)}, u32[]{:S(2)}, u32[]{:S(2)}) %collective-permute-start.11) | collective-permute-done | bytes 32800 | tf_op jit(solution)/shard_map/ppermute | solution.py:13
  64.0 0.9 convolution_convert_fusion.1
  64.9 1.1 %reshape.26 = f32[2,3,32,4,64]{4,3,2,1,0:T(4,128)S(1)} reshape(bf16[2,3,32,256]{3,2,1,0:T(8,128)(2,1)} %convolution_convert_fusion.1) | data formatting | bytes 294912 | tf_op jit(solution)/shard_map/reshape | solution.py:50
  66.0 0.9 multiply_reduce_fusion
  66.9 0.9 reshape.30
  67.8 28.6 %all_gather.4 = bf16[8,2,3,2048]{3,1,2,0:T(2,128)(2,1)S(1)} all-gather(bf16[1,2,3,2048]{3,1,2,0:T(2,128)(2,1)S(1)} %copy.79), channel_id=1, replica_groups=mesh['bias'=8,'gx'=8,'gy'=8] {'bias'}, dimensions={0}, use_global_device_ids=true | all-gather | bytes 221184 | tf_op jit(solution)/shard_map/all_gather | solution.py:53
  96.5 0.2 reduce_sum.22
  96.7 0.6 dynamic-slice_convert_fusion
  (21 shorter events, 0.1 us)
Async XLA Ops:
  0.6 1.9 %copy-start = (bf16[1,2,3,4,256,256]{5,4,3,2,1,0:T(8,128)(2,1)S(1)}, bf16[1,2,3,4,256,256]{5,4,3,2,1,0:T(8,128)(2,1)}, u32[]{:S(2)}) copy-start(bf16[1,2,3,4,256,256]{5,4,3,2,1,0:T(8,128)(2,1)} %param.6) | copy-start | bytes 9437188
  5.2 16.8 %collective-permute-start = (bf16[1,3,32,256]{3,2,1,0:T(8,128)(2,1)}, bf16[1,3,32,256]{3,2,1,0:T(8,128)(2,1)}, u32[]{:S(2)}, u32[]{:S(2)}) collective-permute-start(bf16[1,3,32,256]{3,2,1,0:T(8,128)(2,1)} %get-tuple-element.24), channel_id=1, source_target_pairs={{0,8},{8,16},{16,24},{24,32},{32,40},{40,48},{48,56},{1,9},{9,17},... | collective-permute-start | bytes 147464 | tf_op jit(solution)/shard_map/ppermute | solution.py:13
  7.1 14.9 %collective-permute-start.1 = (bf16[1,3,32,256]{3,2,1,0:T(8,128)(2,1)}, bf16[1,3,32,256]{3,2,1,0:T(8,128)(2,1)}, u32[]{:S(2)}, u32[]{:S(2)}) collective-permute-start(bf16[1,3,32,256]{3,2,1,0:T(8,128)(2,1)} %get-tuple-element.25), channel_id=1, source_target_pairs={{8,0},{16,8},{24,16},{32,24},{40,32},{48,40},{56,48},{9,1},{17,9},... | collective-permute-start | bytes 147464 | tf_op jit(solution)/shard_map/ppermute | solution.py:13
  13.5 7.3 %collective-permute-start.3 = (bf16[2,1,32,256]{3,2,0,1:T(8,128)(2,1)}, bf16[2,1,32,256]{3,2,0,1:T(8,128)(2,1)}, u32[]{:S(2)}, u32[]{:S(2)}) collective-permute-start(bf16[2,1,32,256]{3,2,0,1:T(8,128)(2,1)} %get-tuple-element.20), channel_id=1, source_target_pairs={{1,0},{2,1},{3,2},{4,3},{5,4},{6,5},{7,6},{9,8},{10,9},{11,10},{12... | collective-permute-start | bytes 98312 | tf_op jit(solution)/shard_map/ppermute | solution.py:13
  15.9 6.1 %collective-permute-start.2 = (bf16[2,1,32,256]{3,2,1,0:T(8,128)(2,1)}, bf16[2,1,32,256]{3,2,1,0:T(8,128)(2,1)}, u32[]{:S(2)}, u32[]{:S(2)}) collective-permute-start(bf16[2,1,32,256]{3,2,1,0:T(8,128)(2,1)} %get-tuple-element.21), channel_id=1, source_target_pairs={{0,1},{1,2},{2,3},{3,4},{4,5},{5,6},{6,7},{8,9},{9,10},{10,11},{11... | collective-permute-start | bytes 98312 | tf_op jit(solution)/shard_map/ppermute | solution.py:13
  20.8 22.7 %copy-start.1 = (bf16[1,2,3,256,256]{4,3,2,1,0:T(8,128)(2,1)S(1)}, bf16[1,2,3,256,256]{4,3,2,1,0:T(8,128)(2,1)}, u32[]{:S(2)}) copy-start(bf16[1,2,3,256,256]{4,3,2,1,0:T(8,128)(2,1)} %param.5) | copy-start | bytes 2359300
  24.3 39.6 %copy-start.2 = (bf16[1,2,3,32,256]{4,3,2,1,0:T(8,128)(2,1)S(1)}, bf16[1,2,3,32,256]{4,3,2,1,0:T(8,128)(2,1)}, u32[]{:S(2)}) copy-start(bf16[1,2,3,32,256]{4,3,2,1,0:T(8,128)(2,1)} %param.4) | copy-start | bytes 294916
  24.3 19.1 %collective-permute-start.4 = (bf16[1,3,32,256]{3,2,0,1:T(8,128)(2,1)S(1)}, bf16[1,3,32,256]{3,2,0,1:T(8,128)(2,1)S(1)}, u32[]{:S(2)}, u32[]{:S(2)}) collective-permute-start(bf16[1,3,32,256]{3,2,0,1:T(8,128)(2,1)S(1)} %get-tuple-element.16), channel_id=1, source_target_pairs={{0,8},{8,16},{16,24},{24,32},{32,40},{40,48},{48,56},{1,9},{9,17},... | collective-permute-start | bytes 147464 | tf_op jit(solution)/shard_map/ppermute | solution.py:13
  26.4 17.0 %collective-permute-start.5 = (bf16[1,3,32,256]{3,2,0,1:T(8,128)(2,1)S(1)}, bf16[1,3,32,256]{3,2,0,1:T(8,128)(2,1)S(1)}, u32[]{:S(2)}, u32[]{:S(2)}) collective-permute-start(bf16[1,3,32,256]{3,2,0,1:T(8,128)(2,1)S(1)} %get-tuple-element.17), channel_id=1, source_target_pairs={{8,0},{16,8},{24,16},{32,24},{40,32},{48,40},{56,48},{9,1},{17,9},... | collective-permute-start | bytes 147464 | tf_op jit(solution)/shard_map/ppermute | solution.py:13
  32.2 5.9 %collective-permute-start.6 = (bf16[2,1,32,256]{3,2,0,1:T(8,128)(2,1)S(1)}, bf16[2,1,32,256]{3,2,0,1:T(8,128)(2,1)S(1)}, u32[]{:S(2)}, u32[]{:S(2)}) collective-permute-start(bf16[2,1,32,256]{3,2,0,1:T(8,128)(2,1)S(1)} %get-tuple-element.13), channel_id=1, source_target_pairs={{0,1},{1,2},{2,3},{3,4},{4,5},{5,6},{6,7},{8,9},{9,10},{10,11},{11... | collective-permute-start | bytes 98312 | tf_op jit(solution)/shard_map/ppermute | solution.py:13
  36.1 7.3 %collective-permute-start.7 = (bf16[2,1,32,256]{3,2,1,0:T(8,128)(2,1)S(1)}, bf16[2,1,32,256]{3,2,1,0:T(8,128)(2,1)S(1)}, u32[]{:S(2)}, u32[]{:S(2)}) collective-permute-start(bf16[2,1,32,256]{3,2,1,0:T(8,128)(2,1)S(1)} %get-tuple-element.12), channel_id=1, source_target_pairs={{1,0},{2,1},{3,2},{4,3},{5,4},{6,5},{7,6},{9,8},{10,9},{11,10},{12... | collective-permute-start | bytes 98312 | tf_op jit(solution)/shard_map/ppermute | solution.py:13
  45.3 18.6 %collective-permute-start.8 = (bf16[1,3,32,256]{3,2,0,1:T(8,128)(2,1)S(1)}, bf16[1,3,32,256]{3,2,0,1:T(8,128)(2,1)S(1)}, u32[]{:S(2)}, u32[]{:S(2)}) collective-permute-start(bf16[1,3,32,256]{3,2,0,1:T(8,128)(2,1)S(1)} %get-tuple-element.8), channel_id=1, source_target_pairs={{0,8},{8,16},{16,24},{24,32},{32,40},{40,48},{48,56},{1,9},{9,17},... | collective-permute-start | bytes 147464 | tf_op jit(solution)/shard_map/ppermute | solution.py:13
  47.2 16.7 %collective-permute-start.9 = (bf16[1,3,32,256]{3,2,0,1:T(8,128)(2,1)S(1)}, bf16[1,3,32,256]{3,2,0,1:T(8,128)(2,1)S(1)}, u32[]{:S(2)}, u32[]{:S(2)}) collective-permute-start(bf16[1,3,32,256]{3,2,0,1:T(8,128)(2,1)S(1)} %get-tuple-element.9), channel_id=1, source_target_pairs={{8,0},{16,8},{24,16},{32,24},{40,32},{48,40},{56,48},{9,1},{17,9},... | collective-permute-start | bytes 147464 | tf_op jit(solution)/shard_map/ppermute | solution.py:13
  53.0 7.1 %collective-permute-start.10 = (bf16[2,1,32,256]{3,2,0,1:T(8,128)(2,1)S(1)}, bf16[2,1,32,256]{3,2,0,1:T(8,128)(2,1)S(1)}, u32[]{:S(2)}, u32[]{:S(2)}) collective-permute-start(bf16[2,1,32,256]{3,2,0,1:T(8,128)(2,1)S(1)} %get-tuple-element.5), channel_id=1, source_target_pairs={{0,1},{1,2},{2,3},{3,4},{4,5},{5,6},{6,7},{8,9},{9,10},{10,11},{11... | collective-permute-start | bytes 98312 | tf_op jit(solution)/shard_map/ppermute | solution.py:13
  58.1 5.8 %collective-permute-start.11 = (bf16[2,1,32,256]{3,2,1,0:T(8,128)(2,1)S(1)}, bf16[2,1,32,256]{3,2,1,0:T(8,128)(2,1)S(1)}, u32[]{:S(2)}, u32[]{:S(2)}) collective-permute-start(bf16[2,1,32,256]{3,2,1,0:T(8,128)(2,1)S(1)} %get-tuple-element.4), channel_id=1, source_target_pairs={{1,0},{2,1},{3,2},{4,3},{5,4},{6,5},{7,6},{9,8},{10,9},{11,10},{12... | collective-permute-start | bytes 98312 | tf_op jit(solution)/shard_map/ppermute | solution.py:13
